TPU v7x, 512 devices: a whole 4x8x8 slice. The times are simulated.
512 devices in a mesh: area: 128 (over z, y, core), nrn: 4 (over x).
Axes of the slice: x: 4, y: 8, z: 8, core: 2. Of those that a mesh axis runs over, the one named last changes fastest.
Arguments:
- history: float32 [4, 65536, 128], P(None, ('area', 'nrn')), may hold values from -1 to 1
- drive: float32 [65536, 128], P(('area', 'nrn')), may hold values from -6 to 6
- leak: float32 [65536], P(('area', 'nrn')), may hold values from 0.1 to 0.9
- w_local: float32 [65536, 512], P(('area', 'nrn')), may hold values from -0.25 to 0.25
- w_long: float32 [65536, 4, 1152], P(('area', 'nrn')), may hold values from -0.1875 to 0.1875
- sender_rows: int32 [512, 128, 9], P(('area', 'nrn')), may hold values from 0 to 127
- delays: int32 [128, 128], P('area'), may hold values from 1 to 4
- area_sizes: int32 [128], P('area'), may hold values from 256 to 512, as said below
Outputs:
- rates: float32 [65536, 128], P(('area', 'nrn'))
Inputs may be any that keep to these rules, and one draw needn't show every extreme that they name: `area_sizes`: every area has at least half of its 512 slots live; some area has all of them live, some exactly half. `sender_rows`: indices may repeat.
All inputs are finite; a program needn't handle non-finite values.
Results may differ from a plain program's by a relative error of at most 0.0018.
Values may be sent and summed in bfloat16 or wider, within the bound.
A program may use at most 64 MiB of HBM per device.

v0:
```python
import jax
import jax.numpy as jnp
from jax import lax
from jax.sharding import PartitionSpec as P

STEPS = 6


def cut_along(x, dim, peers):
    lengths = x.shape
    pieces = x.reshape(*lengths[:dim], peers, lengths[dim] // peers, *lengths[dim + 1 :])
    return jnp.moveaxis(pieces, dim, 0)


def sum_at_owner(x, axis, dim):
    peers = lax.axis_size(axis)
    pieces = lax.all_to_all(cut_along(x, dim, peers), axis, 0, 0, tiled=True)
    return jnp.sum(pieces, axis=0)


def unround(values):
    return lax.optimization_barrier(values).astype(jnp.float32)


def local(history, drive, leak, w_local, w_long, sender_rows, delays, area_sizes):
    history_depth, block_rows, stimuli = history.shape
    nrn_count = lax.axis_size("nrn")
    area_count = sender_rows.shape[1]
    proj_count = sender_rows.shape[2]
    offsets = lax.axis_index("nrn") * block_rows + jnp.arange(block_rows, dtype=jnp.int32)
    active = (offsets < area_sizes[0]).astype(jnp.float32)[:, None]
    states = history * active[None]
    picked = ((delays[0] - 1)[:, None] * block_rows + sender_rows[0]).reshape(-1)
    grouped = lax.all_to_all(w_long, "nrn", split_axis=1, concat_axis=0, tiled=True).reshape(
        nrn_count * block_rows, -1
    )
    for iteration in range(STEPS):
        flat_states = states.reshape(history_depth * block_rows, stimuli)
        outgoing = flat_states[picked].astype(jnp.bfloat16).reshape(area_count, proj_count, stimuli)
        incoming = lax.all_to_all(outgoing, "area", split_axis=0, concat_axis=0, tiled=True)
        current = states[0].astype(jnp.bfloat16)
        local_all = lax.all_gather(current, "nrn", axis=0, tiled=True)
        sources = unround(incoming).reshape(-1, stimuli)
        long_term = sum_at_owner(
            jnp.dot(
                grouped,
                sources,
                precision=lax.Precision.HIGHEST,
                preferred_element_type=jnp.float32,
            ),
            "nrn",
            0,
        )
        inputs = (
            long_term
            + jnp.dot(
                w_local,
                unround(local_all),
                precision=lax.Precision.HIGHEST,
                preferred_element_type=jnp.float32,
            )
            + drive
        )
        updated = active * (states[0] + leak[:, None] * (jnp.tanh(inputs) - states[0]))
        states = jnp.concatenate([updated[None], states[:-1]], axis=0)
    return states[0]


def solution(mesh):
    placed = (
        P(None, ("area", "nrn"), None),
        P(("area", "nrn"), None),
        P(("area", "nrn")),
        P(("area", "nrn"), None),
        P(("area", "nrn"), None, None),
        P(("area", "nrn"), None, None),
        P("area", None),
        P("area"),
    )
    return jax.shard_map(
        local, mesh=mesh, in_specs=placed, out_specs=P(("area", "nrn"), None), check_vma=False
    )
```

profile of v0, /device:TPU:8, one launch (start us, length us, event | category | flops | bytes accessed | tf_op | source)
XLA Modules:
  0.0 353.5 jit_solution(10322337798542457753)
XLA Ops:
  7.2 17.4 %all-to-all-start = ((bf16[128,9,128]{2,1,0:T(8,128)(2,1)}), bf16[128,9,128]{2,1,0:T(8,128)(2,1)S(1)}, u32[]{:S(2)}, u32[]{:S(2)}) async-start(bf16[128,9,128]{2,1,0:T(8,128)(2,1)} %convert_element_type.85), calls=%async_computation | async-start | bytes 1048576 | tf_op jit(solution)/shard_map/all_to_all | solution.py:40
  26.2 18.6 %all-to-all-done = bf16[128,9,128]{2,1,0:T(8,128)(2,1)S(1)} async-done(((bf16[128,9,128]{2,1,0:T(8,128)(2,1)}), bf16[128,9,128]{2,1,0:T(8,128)(2,1)S(1)}, u32[]{:S(2)}, u32[]{:S(2)}) %all-to-all-start) | async-done | bytes 294944 | tf_op jit(solution)/shard_map/all_to_all | solution.py:40
  44.8 4.3 %all-to-all-start.1 = ((f32[128,4,1152]{2,0,1:T(8,128)}), f32[128,4,1152]{2,0,1:T(8,128)S(1)}, u32[]{:S(2)}, u32[]{:S(2)}) async-start(f32[128,4,1152]{2,0,1:T(8,128)} %copy.14), calls=%async_computation.1 | async-start | bytes 4718592 | tf_op jit(solution)/shard_map/all_to_all | solution.py:34
  50.6 27.7 %all-to-all-done.1 = f32[128,4,1152]{2,0,1:T(8,128)S(1)} async-done(((f32[128,4,1152]{2,0,1:T(8,128)}), f32[128,4,1152]{2,0,1:T(8,128)S(1)}, u32[]{:S(2)}, u32[]{:S(2)}) %all-to-all-start.1) | async-done | bytes 2359328 | tf_op jit(solution)/shard_map/all_to_all | solution.py:34
  81.5 3.4 all-to-all-start.2
  84.9 13.0 %all_gather.18 = bf16[512,128]{1,0:T(8,128)(2,1)S(1)} all-gather(bf16[128,128]{1,0:T(8,128)(2,1)S(1)} %fusion.46), channel_id=1, replica_groups=mesh['area'=128,'nrn'=4] {'nrn'}, dimensions={0}, use_global_device_ids=true | all-gather | bytes 163840 | tf_op jit(solution)/shard_map/all_gather | solution.py:42
  99.0 2.9 gather_fusion.1
  102.0 27.2 %all_to_all.75 = bf16[128,9,128]{2,1,0:T(8,128)(2,1)} all-to-all(bf16[128,9,128]{2,1,0:T(8,128)(2,1)S(1)} %convert_element_type.88), channel_id=1, replica_groups=mesh['area'=128,'nrn'=4] {'area'}, dimensions={0} | all-to-all | bytes 589824 | tf_op jit(solution)/shard_map/all_to_all | solution.py:40
  132.6 3.4 all-to-all-start.4
  136.0 13.8 %all_gather.19 = bf16[512,128]{1,0:T(8,128)(2,1)S(1)} all-gather(bf16[128,128]{1,0:T(8,128)(2,1)S(1)} %get-tuple-element.5), channel_id=1, replica_groups=mesh['area'=128,'nrn'=4] {'nrn'}, dimensions={0}, use_global_device_ids=true | all-gather | bytes 163840 | tf_op jit(solution)/shard_map/all_gather | solution.py:42
  150.9 2.9 gather_fusion.2
  154.0 25.9 %all_to_all.76 = bf16[128,9,128]{2,1,0:T(8,128)(2,1)} all-to-all(bf16[128,9,128]{2,1,0:T(8,128)(2,1)S(1)} %convert_element_type.91), channel_id=1, replica_groups=mesh['area'=128,'nrn'=4] {'area'}, dimensions={0} | all-to-all | bytes 589824 | tf_op jit(solution)/shard_map/all_to_all | solution.py:40
  183.3 3.4 all-to-all-start.6
  186.7 13.8 %all_gather.20 = bf16[512,128]{1,0:T(8,128)(2,1)S(1)} all-gather(bf16[128,128]{1,0:T(8,128)(2,1)S(1)} %get-tuple-element.7), channel_id=1, replica_groups=mesh['area'=128,'nrn'=4] {'nrn'}, dimensions={0}, use_global_device_ids=true | all-gather | bytes 163840 | tf_op jit(solution)/shard_map/all_gather | solution.py:42
  201.6 2.9 gather_fusion.3
  204.6 25.9 %all_to_all.77 = bf16[128,9,128]{2,1,0:T(8,128)(2,1)} all-to-all(bf16[128,9,128]{2,1,0:T(8,128)(2,1)S(1)} %convert_element_type.94), channel_id=1, replica_groups=mesh['area'=128,'nrn'=4] {'area'}, dimensions={0} | all-to-all | bytes 589824 | tf_op jit(solution)/shard_map/all_to_all | solution.py:40
  234.0 3.4 all-to-all-start.8
  237.4 13.8 %all_gather.21 = bf16[512,128]{1,0:T(8,128)(2,1)S(1)} all-gather(bf16[128,128]{1,0:T(8,128)(2,1)S(1)} %get-tuple-element.9), channel_id=1, replica_groups=mesh['area'=128,'nrn'=4] {'nrn'}, dimensions={0}, use_global_device_ids=true | all-gather | bytes 163840 | tf_op jit(solution)/shard_map/all_gather | solution.py:42
  255.3 25.9 %all_to_all.78 = bf16[128,9,128]{2,1,0:T(8,128)(2,1)} all-to-all(bf16[128,9,128]{2,1,0:T(8,128)(2,1)S(1)} %convert_element_type.97), channel_id=1, replica_groups=mesh['area'=128,'nrn'=4] {'area'}, dimensions={0} | all-to-all | bytes 589824 | tf_op jit(solution)/shard_map/all_to_all | solution.py:40
  284.7 3.4 all-to-all-start.10
  288.1 13.7 %all_gather.22 = bf16[512,128]{1,0:T(8,128)(2,1)S(1)} all-gather(bf16[128,128]{1,0:T(8,128)(2,1)S(1)} %get-tuple-element.11), channel_id=1, replica_groups=mesh['area'=128,'nrn'=4] {'nrn'}, dimensions={0}, use_global_device_ids=true | all-gather | bytes 163840 | tf_op jit(solution)/shard_map/all_gather | solution.py:42
  305.9 25.9 %all_to_all.79 = bf16[128,9,128]{2,1,0:T(8,128)(2,1)} all-to-all(bf16[128,9,128]{2,1,0:T(8,128)(2,1)S(1)} %convert_element_type.100), channel_id=1, replica_groups=mesh['area'=128,'nrn'=4] {'area'}, dimensions={0} | all-to-all | bytes 589824 | tf_op jit(solution)/shard_map/all_to_all | solution.py:40
  335.2 3.4 all-to-all-start.12
  338.6 13.8 %all_gather.23 = bf16[512,128]{1,0:T(8,128)(2,1)S(1)} all-gather(bf16[128,128]{1,0:T(8,128)(2,1)S(1)} %get-tuple-element.13), channel_id=1, replica_groups=mesh['area'=128,'nrn'=4] {'nrn'}, dimensions={0}, use_global_device_ids=true | all-gather | bytes 163840 | tf_op jit(solution)/shard_map/all_gather | solution.py:42
  (116 shorter events, 42.2 us)
Async XLA Ops:
  0.0 98.0 %copy-start = (f32[128,512]{1,0:T(8,128)S(1)}, f32[128,512]{1,0:T(8,128)}, u32[]{:S(2)}) copy-start(f32[128,512]{1,0:T(8,128)} %param.11) | copy-start | bytes 786436
  3.8 20.8 %copy-start.1 = (f32[128,4,1152]{2,1,0:T(4,128)S(1)}, f32[128,4,1152]{2,1,0:T(4,128)}, u32[]{:S(2)}) copy-start(f32[128,4,1152]{2,1,0:T(4,128)} %param.12) | copy-start | bytes 7077892
  7.2 37.6 %all-to-all-start = ((bf16[128,9,128]{2,1,0:T(8,128)(2,1)}), bf16[128,9,128]{2,1,0:T(8,128)(2,1)S(1)}, u32[]{:S(2)}, u32[]{:S(2)}) async-start(bf16[128,9,128]{2,1,0:T(8,128)(2,1)} %convert_element_type.85), calls=%async_computation | async-start | bytes 1048576 | tf_op jit(solution)/shard_map/all_to_all | solution.py:40
  44.8 33.5 %all-to-all-start.1 = ((f32[128,4,1152]{2,0,1:T(8,128)}), f32[128,4,1152]{2,0,1:T(8,128)S(1)}, u32[]{:S(2)}, u32[]{:S(2)}) async-start(f32[128,4,1152]{2,0,1:T(8,128)} %copy.14), calls=%async_computation.1 | async-start | bytes 4718592 | tf_op jit(solution)/shard_map/all_to_all | solution.py:34
  50.6 47.4 %copy-start.2 = (f32[128,128]{1,0:T(8,128)S(1)}, f32[128,128]{1,0:T(8,128)}, u32[]{:S(2)}) copy-start(f32[128,128]{1,0:T(8,128)} %param.9) | copy-start | bytes 196612
  50.6 47.4 %copy-start.21 = (f32[128]{0:T(128)S(1)}, f32[128]{0:T(128)}, u32[]{:S(2)}) copy-start(f32[128]{0:T(128)} %param.10) | copy-start | bytes 1540
  78.3 20.0 %copy-start.11 = (bf16[3,128,128]{2,1,0:T(8,128)(2,1)S(1)}, bf16[3,128,128]{2,1,0:T(8,128)(2,1)}, u32[]{:S(2)}) copy-start(bf16[3,128,128]{2,1,0:T(8,128)(2,1)} %slice.39) | copy-start | bytes 294916
  81.5 16.4 %all-to-all-start.2 = ((f32[4,128,128]{1,2,0:T(8,128)}), f32[4,128,128]{1,2,0:T(8,128)S(1)}, u32[]{:S(2)}, u32[]{:S(2)}) async-start(f32[4,128,128]{1,2,0:T(8,128)} %bitcast.180), calls=%async_computation.2 | async-start | bytes 524288 | tf_op jit(solution)/shard_map/all_to_all | solution.py:17
  129.2 20.6 %copy-start.4 = (f32[128,128]{1,0:T(8,128)S(1)}, f32[128,128]{1,0:T(8,128)}, u32[]{:S(2)}) copy-start(f32[128,128]{1,0:T(8,128)} %copy-done.3) | copy-start | bytes 196612
  129.2 20.6 %copy-start.12 = (bf16[3,128,128]{2,1,0:T(8,128)(2,1)S(1)}, bf16[3,128,128]{2,1,0:T(8,128)(2,1)}, u32[]{:S(2)}) copy-start(bf16[3,128,128]{2,1,0:T(8,128)(2,1)} %slice.39) | copy-start | bytes 294916
  132.6 17.3 %all-to-all-start.4 = ((f32[4,128,128]{1,2,0:T(8,128)}), f32[4,128,128]{1,2,0:T(8,128)S(1)}, u32[]{:S(2)}, u32[]{:S(2)}) async-start(f32[4,128,128]{1,2,0:T(8,128)} %bitcast.179), calls=%async_computation.4 | async-start | bytes 524288 | tf_op jit(solution)/shard_map/all_to_all | solution.py:17
  179.9 20.6 %copy-start.6 = (f32[128,128]{1,0:T(8,128)S(1)}, f32[128,128]{1,0:T(8,128)}, u32[]{:S(2)}) copy-start(f32[128,128]{1,0:T(8,128)} %copy-done.5) | copy-start | bytes 196612
  179.9 20.6 %copy-start.14 = (bf16[3,128,128]{2,1,0:T(8,128)(2,1)S(1)}, bf16[3,128,128]{2,1,0:T(8,128)(2,1)}, u32[]{:S(2)}) copy-start(bf16[3,128,128]{2,1,0:T(8,128)(2,1)} %copy-done.13) | copy-start | bytes 294916
  183.3 17.2 %all-to-all-start.6 = ((f32[4,128,128]{1,2,0:T(8,128)}), f32[4,128,128]{1,2,0:T(8,128)S(1)}, u32[]{:S(2)}, u32[]{:S(2)}) async-start(f32[4,128,128]{1,2,0:T(8,128)} %bitcast.178), calls=%async_computation.6 | async-start | bytes 524288 | tf_op jit(solution)/shard_map/all_to_all | solution.py:17
  200.5 0.6 copy-start.15
  230.6 20.6 %copy-start.8 = (f32[128,128]{1,0:T(8,128)S(1)}, f32[128,128]{1,0:T(8,128)}, u32[]{:S(2)}) copy-start(f32[128,128]{1,0:T(8,128)} %copy-done.7) | copy-start | bytes 196612
  230.6 20.6 %copy-start.16 = (bf16[3,128,128]{2,1,0:T(8,128)(2,1)S(1)}, bf16[3,128,128]{2,1,0:T(8,128)(2,1)}, u32[]{:S(2)}) copy-start(bf16[3,128,128]{2,1,0:T(8,128)(2,1)} %copy-done.15) | copy-start | bytes 294916
  234.0 17.2 %all-to-all-start.8 = ((f32[4,128,128]{1,2,0:T(8,128)}), f32[4,128,128]{1,2,0:T(8,128)S(1)}, u32[]{:S(2)}, u32[]{:S(2)}) async-start(f32[4,128,128]{1,2,0:T(8,128)} %bitcast.177), calls=%async_computation.8 | async-start | bytes 524288 | tf_op jit(solution)/shard_map/all_to_all | solution.py:17
  251.2 0.6 copy-start.17
  281.3 20.5 %copy-start.10 = (f32[128,128]{1,0:T(8,128)S(1)}, f32[128,128]{1,0:T(8,128)}, u32[]{:S(2)}) copy-start(f32[128,128]{1,0:T(8,128)} %copy-done.9) | copy-start | bytes 196612
  281.3 20.5 %copy-start.18 = (bf16[3,128,128]{2,1,0:T(8,128)(2,1)S(1)}, bf16[3,128,128]{2,1,0:T(8,128)(2,1)}, u32[]{:S(2)}) copy-start(bf16[3,128,128]{2,1,0:T(8,128)(2,1)} %copy-done.17) | copy-start | bytes 294916
  284.7 17.2 %all-to-all-start.10 = ((f32[4,128,128]{1,2,0:T(8,128)}), f32[4,128,128]{1,2,0:T(8,128)S(1)}, u32[]{:S(2)}, u32[]{:S(2)}) async-start(f32[4,128,128]{1,2,0:T(8,128)} %bitcast.176), calls=%async_computation.10 | async-start | bytes 524288 | tf_op jit(solution)/shard_map/all_to_all | solution.py:17
  333.0 19.5 %copy-start.20 = (f32[128,128]{1,0:T(8,128)S(1)}, f32[128,128]{1,0:T(8,128)}, u32[]{:S(2)}) copy-start(f32[128,128]{1,0:T(8,128)} %copy-done.19) | copy-start | bytes 196612
  335.2 17.2 %all-to-all-start.12 = ((f32[4,128,128]{1,2,0:T(8,128)}), f32[4,128,128]{1,2,0:T(8,128)S(1)}, u32[]{:S(2)}, u32[]{:S(2)}) async-start(f32[4,128,128]{1,2,0:T(8,128)} %bitcast.175), calls=%async_computation.12 | async-start | bytes 524288 | tf_op jit(solution)/shard_map/all_to_all | solution.py:17
  (6 other events, 3.8 us)
where the time goes:
time: 355 us; the launch traced here: 353 us
  blocking collectives  213 us (60%)
  waiting for transfers between devices  46.3 us (13%)
  starting transfers between devices  42.1 us (12%)
  local copies, waits for them, and re-layouts  37 us (10%)
  matrix products  12 us (3%)
    all_to_all x5, blocking collectives, local(): lax.all_to_all(outgoing, 'area', split_axis=0, concat_axis=0, tiled=True)  131 us
    all_gather x6, blocking collectives, local(): local_all = lax.all_gather(current, 'nrn', axis=0, tiled=True)  81.9 us
    all_to_all x1, waiting for transfers between devices, local(): lax.all_to_all(w_long, 'nrn', split_axis=1, concat_axis=0, tiled=True)  27.7 us
    all_to_all x6, starting transfers between devices, sum_at_owner(): pieces = lax.all_to_all(cut_along(x, dim, peers), axis, 0, 0, tiled=True)  20.4 us
    all_to_all x1, waiting for transfers between devices, local(): lax.all_to_all(outgoing, 'area', split_axis=0, concat_axis=0, tiled=True)  18.6 us
    all_to_all x1, starting transfers between devices, local(): lax.all_to_all(outgoing, 'area', split_axis=0, concat_axis=0, tiled=True)  17.4 us
    gather x6, local copies, waits for them, and re-layouts, local(): flat_states[picked].astype(jnp.bfloat16)  17.1 us
    dot_general x6, matrix products, local(): jnp.dot(grouped, sources, precision=lax.Precision.HIGHEST, preferred_elem...  9.74 us
  transfers between devices with their start and end apart: 8, of which 2 were waited for; matrix products, arithmetic and copies ran while one was open for 1% of the time, Pallas kernels for 0%

commit v1 on v0

--- a/solution.py
+++ b/solution.py
@@ -4,6 +4,32 @@
 from jax.sharding import PartitionSpec as P
 
 STEPS = 6
+
+
+def positions_state(tile_in, dim_k):
+    tile_in = jnp.moveaxis(tile_in, 0, dim_k)
+    y2 = tile_in.shape
+    return tile_in.reshape(*y2[:dim_k], y2[dim_k] * y2[dim_k + 1], *y2[dim_k + 2 :])
+
+
+def time_thing(z, row_axis, in_dim=0):
+    many = jax.lax.axis_size(row_axis)
+    lanes = [(src_i, (src_i + 1) % many) for src_i in range(many)]
+    arrivals = [(i0, ii) for ii, i0 in lanes]
+    last, r2 = ([], [])
+    for dd in [*range(many - 1)]:
+        if dd % 2 == 0:
+            mid_arr = jax.lax.ppermute(last[-1] if last else z, row_axis, lanes)
+            last.append(mid_arr)
+        else:
+            extra = jax.lax.ppermute(r2[-1] if r2 else z, row_axis, arrivals)
+            r2.append(extra)
+    odd = jnp.stack([*last[::-1], z, *r2])
+    passed = jax.lax.axis_index(row_axis)
+    piece_out = len(last)
+    step_out = passed - piece_out
+    odd = odd[(jnp.arange(many) - step_out) % many]
+    return positions_state(odd, in_dim)
 
 
 def cut_along(x, dim, peers):
@@ -39,7 +65,7 @@
         outgoing = flat_states[picked].astype(jnp.bfloat16).reshape(area_count, proj_count, stimuli)
         incoming = lax.all_to_all(outgoing, "area", split_axis=0, concat_axis=0, tiled=True)
         current = states[0].astype(jnp.bfloat16)
-        local_all = lax.all_gather(current, "nrn", axis=0, tiled=True)
+        local_all = time_thing(current, "nrn")
         sources = unround(incoming).reshape(-1, stimuli)
         long_term = sum_at_owner(
             jnp.dot(

time: 355 us -> 330 us (0.930)
  the two profiles are of different devices: /device:TPU:8 before, /device:TPU:1 now
where the time goes in v1:
time: 330 us; the launch traced here: 328 us
  starting transfers between devices  122 us (37%)
  waiting for transfers between devices  118 us (36%)
  local copies, waits for them, and re-layouts  39.9 us (12%)
  blocking collectives  26.3 us (8%)
  matrix products  12.9 us (4%)
  other arithmetic  6.66 us (2%)
    all_to_all x5, waiting for transfers between devices, local(): lax.all_to_all(outgoing, 'area', split_axis=0, concat_axis=0, tiled=True)  67.7 us
    all_to_all x5, starting transfers between devices, local(): lax.all_to_all(outgoing, 'area', split_axis=0, concat_axis=0, tiled=True)  43.9 us
    ppermute x12, starting transfers between devices, time_thing(): mid_arr = jax.lax.ppermute(last[-1] if last else z, row_axis, lanes)  28 us
    all_to_all x1, blocking collectives, local(): lax.all_to_all(outgoing, 'area', split_axis=0, concat_axis=0, tiled=True)  26.3 us
    all_to_all x6, waiting for transfers between devices, sum_at_owner(): pieces = lax.all_to_all(cut_along(x, dim, peers), axis, 0, 0, tiled=True)  25.6 us
    ppermute x6, starting transfers between devices, time_thing(): extra = jax.lax.ppermute(r2[-1] if r2 else z, row_axis, arrivals)  25 us
    ppermute x12, waiting for transfers between devices, time_thing(): mid_arr = jax.lax.ppermute(last[-1] if last else z, row_axis, lanes)  24.9 us
    all_to_all x6, starting transfers between devices, sum_at_owner(): pieces = lax.all_to_all(cut_along(x, dim, peers), axis, 0, 0, tiled=True)  21 us
  transfers between devices with their start and end apart: 30, of which 13 were waited for; matrix products, arithmetic and copies ran while one was open for 7% of the time, Pallas kernels for 0%

profile of v1, /device:TPU:1, one launch (start us, length us, event | category | flops | bytes accessed | tf_op | source)
XLA Modules:
  0.0 327.6 jit_solution(13052577272770913790)
XLA Ops:
  7.2 18.4 %all-to-all-start = ((bf16[128,9,128]{2,1,0:T(8,128)(2,1)}), bf16[128,9,128]{2,1,0:T(8,128)(2,1)S(1)}, u32[]{:S(2)}, u32[]{:S(2)}) async-start(bf16[128,9,128]{2,1,0:T(8,128)(2,1)} %convert_element_type.88), calls=%async_computation | async-start | bytes 1048576 | tf_op jit(solution)/shard_map/all_to_all | solution.py:66
  27.2 19.0 %all-to-all-done = bf16[128,9,128]{2,1,0:T(8,128)(2,1)S(1)} async-done(((bf16[128,9,128]{2,1,0:T(8,128)(2,1)}), bf16[128,9,128]{2,1,0:T(8,128)(2,1)S(1)}, u32[]{:S(2)}, u32[]{:S(2)}) %all-to-all-start) | async-done | bytes 294944 | tf_op jit(solution)/shard_map/all_to_all | solution.py:66
  46.2 4.0 %all-to-all-start.1 = ((f32[128,4,1152]{2,0,1:T(8,128)}), f32[128,4,1152]{2,0,1:T(8,128)S(1)}, u32[]{:S(2)}, u32[]{:S(2)}) async-start(f32[128,4,1152]{2,0,1:T(8,128)} %copy.14), calls=%async_computation.1 | async-start | bytes 4718592 | tf_op jit(solution)/shard_map/all_to_all | solution.py:60
  50.2 4.6 %collective-permute-start.2 = (bf16[128,128]{1,0:T(8,128)(2,1)S(1)}, bf16[128,128]{1,0:T(8,128)(2,1)}, u32[]{:S(2)}, u32[]{:S(2)}) collective-permute-start(bf16[128,128]{1,0:T(8,128)(2,1)S(1)} %get-tuple-element.6), channel_id=1, source_target_pairs={{1,0},{2,1},{3,2},{0,3},{5,4},{6,5},{7,6},{4,7},{9,8},{10,9},{11,1... | collective-permute-start | bytes 98312 | tf_op jit(solution)/shard_map/ppermute | solution.py:25
  57.3 19.6 %collective-permute-done = bf16[128,128]{1,0:T(8,128)(2,1)} collective-permute-done((bf16[128,128]{1,0:T(8,128)(2,1)S(1)}, bf16[128,128]{1,0:T(8,128)(2,1)}, u32[]{:S(2)}, u32[]{:S(2)}) %collective-permute-start) | collective-permute-done | bytes 32800 | tf_op jit(solution)/shard_map/ppermute | solution.py:22
  76.9 4.2 %collective-permute-start.1 = (bf16[128,128]{1,0:T(8,128)(2,1)}, bf16[128,128]{1,0:T(8,128)(2,1)}, u32[]{:S(2)}, u32[]{:S(2)}) collective-permute-start(bf16[128,128]{1,0:T(8,128)(2,1)} %collective-permute-done), channel_id=1, source_target_pairs={{0,1},{1,2},{2,3},{3,0},{4,5},{5,6},{6,7},{7,4},{8,9},{9,10},{10,1... | collective-permute-start | bytes 98312 | tf_op jit(solution)/shard_map/ppermute | solution.py:22
  85.2 4.0 %all-to-all-start.2 = ((f32[4,128,128]{1,2,0:T(8,128)}), f32[4,128,128]{1,2,0:T(8,128)S(1)}, u32[]{:S(2)}, u32[]{:S(2)}) async-start(f32[4,128,128]{1,2,0:T(8,128)} %bitcast.208), calls=%async_computation.2 | async-start | bytes 524288 | tf_op jit(solution)/shard_map/all_to_all | solution.py:43
  100.5 8.5 %all-to-all-start.3 = ((bf16[128,9,128]{2,1,0:T(8,128)(2,1)}), bf16[128,9,128]{2,1,0:T(8,128)(2,1)S(1)}, u32[]{:S(2)}, u32[]{:S(2)}) async-start(bf16[128,9,128]{2,1,0:T(8,128)(2,1)} %convert_element_type.92), calls=%async_computation.3 | async-start | bytes 1048576 | tf_op jit(solution)/shard_map/all_to_all | solution.py:66
  111.2 4.3 %collective-permute-start.5 = (bf16[128,128]{1,0:T(8,128)(2,1)S(1)}, bf16[128,128]{1,0:T(8,128)(2,1)}, u32[]{:S(2)}, u32[]{:S(2)}) collective-permute-start(bf16[128,128]{1,0:T(8,128)(2,1)S(1)} %get-tuple-element.7), channel_id=1, source_target_pairs={{1,0},{2,1},{3,2},{0,3},{5,4},{6,5},{7,6},{4,7},{9,8},{10,9},{11,1... | collective-permute-start | bytes 98312 | tf_op jit(solution)/shard_map/ppermute | solution.py:25
  117.4 12.2 %all-to-all-done.3 = bf16[128,9,128]{2,1,0:T(8,128)(2,1)S(1)} async-done(((bf16[128,9,128]{2,1,0:T(8,128)(2,1)}), bf16[128,9,128]{2,1,0:T(8,128)(2,1)S(1)}, u32[]{:S(2)}, u32[]{:S(2)}) %all-to-all-start.3) | async-done | bytes 294944 | tf_op jit(solution)/shard_map/all_to_all | solution.py:66
  137.0 5.5 %all-to-all-done.4 = f32[4,128,128]{1,2,0:T(8,128)S(1)} async-done(((f32[4,128,128]{1,2,0:T(8,128)}), f32[4,128,128]{1,2,0:T(8,128)S(1)}, u32[]{:S(2)}, u32[]{:S(2)}) %all-to-all-start.4) | async-done | bytes 262176 | tf_op jit(solution)/shard_map/all_to_all | solution.py:43
  147.4 5.8 %all-to-all-start.5 = ((bf16[128,9,128]{2,1,0:T(8,128)(2,1)}), bf16[128,9,128]{2,1,0:T(8,128)(2,1)S(1)}, u32[]{:S(2)}, u32[]{:S(2)}) async-start(bf16[128,9,128]{2,1,0:T(8,128)(2,1)} %convert_element_type.95), calls=%async_computation.5 | async-start | bytes 1048576 | tf_op jit(solution)/shard_map/all_to_all | solution.py:66
  155.4 4.3 %collective-permute-start.8 = (bf16[128,128]{1,0:T(8,128)(2,1)S(1)}, bf16[128,128]{1,0:T(8,128)(2,1)}, u32[]{:S(2)}, u32[]{:S(2)}) collective-permute-start(bf16[128,128]{1,0:T(8,128)(2,1)S(1)} %get-tuple-element.9), channel_id=1, source_target_pairs={{1,0},{2,1},{3,2},{0,3},{5,4},{6,5},{7,6},{4,7},{9,8},{10,9},{11,1... | collective-permute-start | bytes 98312 | tf_op jit(solution)/shard_map/ppermute | solution.py:25
  161.7 12.2 %all-to-all-done.5 = bf16[128,9,128]{2,1,0:T(8,128)(2,1)S(1)} async-done(((bf16[128,9,128]{2,1,0:T(8,128)(2,1)}), bf16[128,9,128]{2,1,0:T(8,128)(2,1)S(1)}, u32[]{:S(2)}, u32[]{:S(2)}) %all-to-all-start.5) | async-done | bytes 294944 | tf_op jit(solution)/shard_map/all_to_all | solution.py:66
  181.3 5.5 %all-to-all-done.6 = f32[4,128,128]{1,2,0:T(8,128)S(1)} async-done(((f32[4,128,128]{1,2,0:T(8,128)}), f32[4,128,128]{1,2,0:T(8,128)S(1)}, u32[]{:S(2)}, u32[]{:S(2)}) %all-to-all-start.6) | async-done | bytes 262176 | tf_op jit(solution)/shard_map/all_to_all | solution.py:43
  191.7 5.6 %all-to-all-start.7 = ((bf16[128,9,128]{2,1,0:T(8,128)(2,1)}), bf16[128,9,128]{2,1,0:T(8,128)(2,1)S(1)}, u32[]{:S(2)}, u32[]{:S(2)}) async-start(bf16[128,9,128]{2,1,0:T(8,128)(2,1)} %convert_element_type.98), calls=%async_computation.7 | async-start | bytes 1048576 | tf_op jit(solution)/shard_map/all_to_all | solution.py:66
  199.5 4.3 %collective-permute-start.11 = (bf16[128,128]{1,0:T(8,128)(2,1)S(1)}, bf16[128,128]{1,0:T(8,128)(2,1)}, u32[]{:S(2)}, u32[]{:S(2)}) collective-permute-start(bf16[128,128]{1,0:T(8,128)(2,1)S(1)} %get-tuple-element.11), channel_id=1, source_target_pairs={{1,0},{2,1},{3,2},{0,3},{5,4},{6,5},{7,6},{4,7},{9,8},{10,9},{11,1... | collective-permute-start | bytes 98312 | tf_op jit(solution)/shard_map/ppermute | solution.py:25
  205.7 12.2 %all-to-all-done.7 = bf16[128,9,128]{2,1,0:T(8,128)(2,1)S(1)} async-done(((bf16[128,9,128]{2,1,0:T(8,128)(2,1)}), bf16[128,9,128]{2,1,0:T(8,128)(2,1)S(1)}, u32[]{:S(2)}, u32[]{:S(2)}) %all-to-all-start.7) | async-done | bytes 294944 | tf_op jit(solution)/shard_map/all_to_all | solution.py:66
  225.3 5.5 %all-to-all-done.8 = f32[4,128,128]{1,2,0:T(8,128)S(1)} async-done(((f32[4,128,128]{1,2,0:T(8,128)}), f32[4,128,128]{1,2,0:T(8,128)S(1)}, u32[]{:S(2)}, u32[]{:S(2)}) %all-to-all-start.8) | async-done | bytes 262176 | tf_op jit(solution)/shard_map/all_to_all | solution.py:43
  235.8 5.6 %all-to-all-start.9 = ((bf16[128,9,128]{2,1,0:T(8,128)(2,1)}), bf16[128,9,128]{2,1,0:T(8,128)(2,1)S(1)}, u32[]{:S(2)}, u32[]{:S(2)}) async-start(bf16[128,9,128]{2,1,0:T(8,128)(2,1)} %convert_element_type.101), calls=%async_computation.9 | async-start | bytes 1048576 | tf_op jit(solution)/shard_map/all_to_all | solution.py:66
  243.6 4.3 %collective-permute-start.14 = (bf16[128,128]{1,0:T(8,128)(2,1)S(1)}, bf16[128,128]{1,0:T(8,128)(2,1)}, u32[]{:S(2)}, u32[]{:S(2)}) collective-permute-start(bf16[128,128]{1,0:T(8,128)(2,1)S(1)} %get-tuple-element.13), channel_id=1, source_target_pairs={{1,0},{2,1},{3,2},{0,3},{5,4},{6,5},{7,6},{4,7},{9,8},{10,9},{11,1... | collective-permute-start | bytes 98312 | tf_op jit(solution)/shard_map/ppermute | solution.py:25
  250.0 12.0 %all-to-all-done.9 = bf16[128,9,128]{2,1,0:T(8,128)(2,1)S(1)} async-done(((bf16[128,9,128]{2,1,0:T(8,128)(2,1)}), bf16[128,9,128]{2,1,0:T(8,128)(2,1)S(1)}, u32[]{:S(2)}, u32[]{:S(2)}) %all-to-all-start.9) | async-done | bytes 294944 | tf_op jit(solution)/shard_map/all_to_all | solution.py:66
  269.4 5.6 %all-to-all-done.10 = f32[4,128,128]{1,2,0:T(8,128)S(1)} async-done(((f32[4,128,128]{1,2,0:T(8,128)}), f32[4,128,128]{1,2,0:T(8,128)S(1)}, u32[]{:S(2)}, u32[]{:S(2)}) %all-to-all-start.10) | async-done | bytes 262176 | tf_op jit(solution)/shard_map/all_to_all | solution.py:43
  279.0 26.3 %all_to_all.75 = bf16[128,9,128]{2,1,0:T(8,128)(2,1)} all-to-all(bf16[128,9,128]{2,1,0:T(8,128)(2,1)S(1)} %convert_element_type.104), channel_id=1, replica_groups=mesh['area'=128,'nrn'=4] {'area'}, dimensions={0} | all-to-all | bytes 589824 | tf_op jit(solution)/shard_map/all_to_all | solution.py:66
  (168 shorter events, 112.2 us)
Async XLA Ops:
  7.2 39.0 %all-to-all-start = ((bf16[128,9,128]{2,1,0:T(8,128)(2,1)}), bf16[128,9,128]{2,1,0:T(8,128)(2,1)S(1)}, u32[]{:S(2)}, u32[]{:S(2)}) async-start(bf16[128,9,128]{2,1,0:T(8,128)(2,1)} %convert_element_type.88), calls=%async_computation | async-start | bytes 1048576 | tf_op jit(solution)/shard_map/all_to_all | solution.py:66
  46.2 35.8 %all-to-all-start.1 = ((f32[128,4,1152]{2,0,1:T(8,128)}), f32[128,4,1152]{2,0,1:T(8,128)S(1)}, u32[]{:S(2)}, u32[]{:S(2)}) async-start(f32[128,4,1152]{2,0,1:T(8,128)} %copy.14), calls=%async_computation.1 | async-start | bytes 4718592 | tf_op jit(solution)/shard_map/all_to_all | solution.py:60
  50.2 38.9 %collective-permute-start.2 = (bf16[128,128]{1,0:T(8,128)(2,1)S(1)}, bf16[128,128]{1,0:T(8,128)(2,1)}, u32[]{:S(2)}, u32[]{:S(2)}) collective-permute-start(bf16[128,128]{1,0:T(8,128)(2,1)S(1)} %get-tuple-element.6), channel_id=1, source_target_pairs={{1,0},{2,1},{3,2},{0,3},{5,4},{6,5},{7,6},{4,7},{9,8},{10,9},{11,1... | collective-permute-start | bytes 98312 | tf_op jit(solution)/shard_map/ppermute | solution.py:25
  54.8 22.1 %collective-permute-start = (bf16[128,128]{1,0:T(8,128)(2,1)S(1)}, bf16[128,128]{1,0:T(8,128)(2,1)}, u32[]{:S(2)}, u32[]{:S(2)}) collective-permute-start(bf16[128,128]{1,0:T(8,128)(2,1)S(1)} %get-tuple-element.6), channel_id=1, source_target_pairs={{0,1},{1,2},{2,3},{3,0},{4,5},{5,6},{6,7},{7,4},{8,9},{9,10},{10,1... | collective-permute-start | bytes 98312 | tf_op jit(solution)/shard_map/ppermute | solution.py:22
  76.9 12.3 %collective-permute-start.1 = (bf16[128,128]{1,0:T(8,128)(2,1)}, bf16[128,128]{1,0:T(8,128)(2,1)}, u32[]{:S(2)}, u32[]{:S(2)}) collective-permute-start(bf16[128,128]{1,0:T(8,128)(2,1)} %collective-permute-done), channel_id=1, source_target_pairs={{0,1},{1,2},{2,3},{3,0},{4,5},{5,6},{6,7},{7,4},{8,9},{9,10},{10,1... | collective-permute-start | bytes 98312 | tf_op jit(solution)/shard_map/ppermute | solution.py:22
  85.2 9.5 %all-to-all-start.2 = ((f32[4,128,128]{1,2,0:T(8,128)}), f32[4,128,128]{1,2,0:T(8,128)S(1)}, u32[]{:S(2)}, u32[]{:S(2)}) async-start(f32[4,128,128]{1,2,0:T(8,128)} %bitcast.208), calls=%async_computation.2 | async-start | bytes 524288 | tf_op jit(solution)/shard_map/all_to_all | solution.py:43
  100.5 29.2 %all-to-all-start.3 = ((bf16[128,9,128]{2,1,0:T(8,128)(2,1)}), bf16[128,9,128]{2,1,0:T(8,128)(2,1)S(1)}, u32[]{:S(2)}, u32[]{:S(2)}) async-start(bf16[128,9,128]{2,1,0:T(8,128)(2,1)} %convert_element_type.92), calls=%async_computation.3 | async-start | bytes 1048576 | tf_op jit(solution)/shard_map/all_to_all | solution.py:66
  111.2 24.3 %collective-permute-start.5 = (bf16[128,128]{1,0:T(8,128)(2,1)S(1)}, bf16[128,128]{1,0:T(8,128)(2,1)}, u32[]{:S(2)}, u32[]{:S(2)}) collective-permute-start(bf16[128,128]{1,0:T(8,128)(2,1)S(1)} %get-tuple-element.7), channel_id=1, source_target_pairs={{1,0},{2,1},{3,2},{0,3},{5,4},{6,5},{7,6},{4,7},{9,8},{10,9},{11,1... | collective-permute-start | bytes 98312 | tf_op jit(solution)/shard_map/ppermute | solution.py:25
  115.5 20.0 %collective-permute-start.4 = (bf16[128,128]{1,0:T(8,128)(2,1)}, bf16[128,128]{1,0:T(8,128)(2,1)}, u32[]{:S(2)}, u32[]{:S(2)}) collective-permute-start(bf16[128,128]{1,0:T(8,128)(2,1)} %collective-permute-done.3), channel_id=1, source_target_pairs={{0,1},{1,2},{2,3},{3,0},{4,5},{5,6},{6,7},{7,4},{8,9},{9,10},{10,1... | collective-permute-start | bytes 98312 | tf_op jit(solution)/shard_map/ppermute | solution.py:22
  132.0 10.6 %all-to-all-start.4 = ((f32[4,128,128]{1,2,0:T(8,128)}), f32[4,128,128]{1,2,0:T(8,128)S(1)}, u32[]{:S(2)}, u32[]{:S(2)}) async-start(f32[4,128,128]{1,2,0:T(8,128)} %bitcast.207), calls=%async_computation.4 | async-start | bytes 524288 | tf_op jit(solution)/shard_map/all_to_all | solution.py:43
  147.4 26.5 %all-to-all-start.5 = ((bf16[128,9,128]{2,1,0:T(8,128)(2,1)}), bf16[128,9,128]{2,1,0:T(8,128)(2,1)S(1)}, u32[]{:S(2)}, u32[]{:S(2)}) async-start(bf16[128,9,128]{2,1,0:T(8,128)(2,1)} %convert_element_type.95), calls=%async_computation.5 | async-start | bytes 1048576 | tf_op jit(solution)/shard_map/all_to_all | solution.py:66
  155.4 24.3 %collective-permute-start.8 = (bf16[128,128]{1,0:T(8,128)(2,1)S(1)}, bf16[128,128]{1,0:T(8,128)(2,1)}, u32[]{:S(2)}, u32[]{:S(2)}) collective-permute-start(bf16[128,128]{1,0:T(8,128)(2,1)S(1)} %get-tuple-element.9), channel_id=1, source_target_pairs={{1,0},{2,1},{3,2},{0,3},{5,4},{6,5},{7,6},{4,7},{9,8},{10,9},{11,1... | collective-permute-start | bytes 98312 | tf_op jit(solution)/shard_map/ppermute | solution.py:25
  159.7 20.0 %collective-permute-start.7 = (bf16[128,128]{1,0:T(8,128)(2,1)}, bf16[128,128]{1,0:T(8,128)(2,1)}, u32[]{:S(2)}, u32[]{:S(2)}) collective-permute-start(bf16[128,128]{1,0:T(8,128)(2,1)} %collective-permute-done.6), channel_id=1, source_target_pairs={{0,1},{1,2},{2,3},{3,0},{4,5},{5,6},{6,7},{7,4},{8,9},{9,10},{10,1... | collective-permute-start | bytes 98312 | tf_op jit(solution)/shard_map/ppermute | solution.py:22
  176.2 10.6 %all-to-all-start.6 = ((f32[4,128,128]{1,2,0:T(8,128)}), f32[4,128,128]{1,2,0:T(8,128)S(1)}, u32[]{:S(2)}, u32[]{:S(2)}) async-start(f32[4,128,128]{1,2,0:T(8,128)} %bitcast.206), calls=%async_computation.6 | async-start | bytes 524288 | tf_op jit(solution)/shard_map/all_to_all | solution.py:43
  191.7 26.3 %all-to-all-start.7 = ((bf16[128,9,128]{2,1,0:T(8,128)(2,1)}), bf16[128,9,128]{2,1,0:T(8,128)(2,1)S(1)}, u32[]{:S(2)}, u32[]{:S(2)}) async-start(bf16[128,9,128]{2,1,0:T(8,128)(2,1)} %convert_element_type.98), calls=%async_computation.7 | async-start | bytes 1048576 | tf_op jit(solution)/shard_map/all_to_all | solution.py:66
  199.5 24.3 %collective-permute-start.11 = (bf16[128,128]{1,0:T(8,128)(2,1)S(1)}, bf16[128,128]{1,0:T(8,128)(2,1)}, u32[]{:S(2)}, u32[]{:S(2)}) collective-permute-start(bf16[128,128]{1,0:T(8,128)(2,1)S(1)} %get-tuple-element.11), channel_id=1, source_target_pairs={{1,0},{2,1},{3,2},{0,3},{5,4},{6,5},{7,6},{4,7},{9,8},{10,9},{11,1... | collective-permute-start | bytes 98312 | tf_op jit(solution)/shard_map/ppermute | solution.py:25
  203.8 20.0 %collective-permute-start.10 = (bf16[128,128]{1,0:T(8,128)(2,1)}, bf16[128,128]{1,0:T(8,128)(2,1)}, u32[]{:S(2)}, u32[]{:S(2)}) collective-permute-start(bf16[128,128]{1,0:T(8,128)(2,1)} %collective-permute-done.9), channel_id=1, source_target_pairs={{0,1},{1,2},{2,3},{3,0},{4,5},{5,6},{6,7},{7,4},{8,9},{9,10},{10,1... | collective-permute-start | bytes 98312 | tf_op jit(solution)/shard_map/ppermute | solution.py:22
  220.3 10.6 %all-to-all-start.8 = ((f32[4,128,128]{1,2,0:T(8,128)}), f32[4,128,128]{1,2,0:T(8,128)S(1)}, u32[]{:S(2)}, u32[]{:S(2)}) async-start(f32[4,128,128]{1,2,0:T(8,128)} %bitcast.205), calls=%async_computation.8 | async-start | bytes 524288 | tf_op jit(solution)/shard_map/all_to_all | solution.py:43
  235.8 26.3 %all-to-all-start.9 = ((bf16[128,9,128]{2,1,0:T(8,128)(2,1)}), bf16[128,9,128]{2,1,0:T(8,128)(2,1)S(1)}, u32[]{:S(2)}, u32[]{:S(2)}) async-start(bf16[128,9,128]{2,1,0:T(8,128)(2,1)} %convert_element_type.101), calls=%async_computation.9 | async-start | bytes 1048576 | tf_op jit(solution)/shard_map/all_to_all | solution.py:66
  243.6 24.3 %collective-permute-start.14 = (bf16[128,128]{1,0:T(8,128)(2,1)S(1)}, bf16[128,128]{1,0:T(8,128)(2,1)}, u32[]{:S(2)}, u32[]{:S(2)}) collective-permute-start(bf16[128,128]{1,0:T(8,128)(2,1)S(1)} %get-tuple-element.13), channel_id=1, source_target_pairs={{1,0},{2,1},{3,2},{0,3},{5,4},{6,5},{7,6},{4,7},{9,8},{10,9},{11,1... | collective-permute-start | bytes 98312 | tf_op jit(solution)/shard_map/ppermute | solution.py:25
  247.9 20.0 %collective-permute-start.13 = (bf16[128,128]{1,0:T(8,128)(2,1)}, bf16[128,128]{1,0:T(8,128)(2,1)}, u32[]{:S(2)}, u32[]{:S(2)}) collective-permute-start(bf16[128,128]{1,0:T(8,128)(2,1)} %collective-permute-done.12), channel_id=1, source_target_pairs={{0,1},{1,2},{2,3},{3,0},{4,5},{5,6},{6,7},{7,4},{8,9},{9,10},{10,1... | collective-permute-start | bytes 98312 | tf_op jit(solution)/shard_map/ppermute | solution.py:22
  264.4 10.5 %all-to-all-start.10 = ((f32[4,128,128]{1,2,0:T(8,128)}), f32[4,128,128]{1,2,0:T(8,128)S(1)}, u32[]{:S(2)}, u32[]{:S(2)}) async-start(f32[4,128,128]{1,2,0:T(8,128)} %bitcast.204), calls=%async_computation.10 | async-start | bytes 524288 | tf_op jit(solution)/shard_map/all_to_all | solution.py:43
  308.7 17.8 %all-to-all-start.12 = ((f32[4,128,128]{1,2,0:T(8,128)}), f32[4,128,128]{1,2,0:T(8,128)S(1)}, u32[]{:S(2)}, u32[]{:S(2)}) async-start(f32[4,128,128]{1,2,0:T(8,128)} %bitcast.203), calls=%async_computation.12 | async-start | bytes 524288 | tf_op jit(solution)/shard_map/all_to_all | solution.py:43
  312.2 7.8 %collective-permute-start.15 = (bf16[128,128]{1,0:T(8,128)(2,1)S(1)}, bf16[128,128]{1,0:T(8,128)(2,1)S(1)}, u32[]{:S(2)}, u32[]{:S(2)}) collective-permute-start(bf16[128,128]{1,0:T(8,128)(2,1)S(1)} %get-tuple-element.15), channel_id=1, source_target_pairs={{0,1},{1,2},{2,3},{3,0},{4,5},{5,6},{6,7},{7,4},{8,9},{9,10},{10,1... | collective-permute-start | bytes 98312 | tf_op jit(solution)/shard_map/ppermute | solution.py:22
  (30 other events, 313.6 us)
